TPU v7x, 32 devices: a whole 2x2x4 slice. The times are simulated.
32 devices in a mesh: dp: 16 (over z, x, core), tensor: 2 (over y).
Axes of the slice: x: 2, y: 2, z: 4, core: 2. Of those that a mesh axis runs over, the one named last changes fastest.
Arguments:
- latent_pre: bfloat16 [8192, 512], P('dp'), may hold values from -6 to 6
- norm_gain: float32 [512], replicated, may hold values from 0.1 to 1.9
- kv_weight: bfloat16 [512, 4096], P(None, 'tensor'), may hold values from -0.25 to 0.25
- down_weight: bfloat16 [7168, 512], P('tensor'), may hold values from -0.25 to 0.25
- grad_kv: bfloat16 [8192, 4096], P('dp', 'tensor'), may hold values from -0.75 to 0.75
- master: float32 [512, 4096], P('dp', 'tensor'), may hold values from -0.25 to 0.25
- first_moment: float32 [512, 4096], P('dp', 'tensor'), may hold values from -120 to 120
- second_moment: float32 [512, 4096], P('dp', 'tensor'), may hold values from 100 to 1000
Outputs:
- grad_hidden: bfloat16 [8192, 7168], P('dp', 'tensor')
- new_master: float32 [512, 4096], P('dp', 'tensor')
- new_first: float32 [512, 4096], P('dp', 'tensor')
- new_second: float32 [512, 4096], P('dp', 'tensor')
- new_replica: bfloat16 [512, 4096], P(None, 'tensor')
All inputs are finite; a program needn't handle non-finite values.
Results may differ from a plain program's by a relative error of at most 0.002.
The roundings to bfloat16 on the way count: a program that leaves them out, or rounds other values in their place, can miss the bound.
Values may be sent and summed in bfloat16 or wider, within the bound.
A program may use at most 64 MiB of HBM per device.

v0:
```python
import jax
import jax.numpy as jnp
from jax import lax
from jax.sharding import PartitionSpec as P

bias_first = 0.9999734386011124
bias_second = 0.09520785288629112


def norm_backward(latent_rows, norm_gain, grad_rows):
    values = latent_rows.astype(jnp.float32)
    inverse_rms = lax.rsqrt(jnp.mean(values * values, axis=1, keepdims=True) + 1e-06)
    unit = values * inverse_rms
    scaled = grad_rows * norm_gain
    inner = jnp.mean(scaled * unit, axis=1, keepdims=True)
    return (inverse_rms * (scaled - unit * inner)).astype(jnp.bfloat16)


def local(
    latent_pre, norm_gain, kv_weight, down_weight, grad_kv, master, first_moment, second_moment
):
    values = latent_pre.astype(jnp.float32)
    inverse_rms = lax.rsqrt(jnp.mean(values * values, axis=1, keepdims=True) + 1e-06)
    normalized = (values * inverse_rms * norm_gain).astype(jnp.bfloat16)
    partial_grad = lax.dot_general(
        grad_kv, kv_weight, (((1,), (1,)), ((), ())), preferred_element_type=jnp.float32
    )
    grad_latent = lax.psum(partial_grad, "tensor")
    grad_pre = norm_backward(latent_pre, norm_gain, grad_latent)
    grad_hidden = lax.dot_general(
        grad_pre, down_weight, (((1,), (1,)), ((), ())), preferred_element_type=jnp.float32
    ).astype(jnp.bfloat16)
    weight_grad = lax.psum_scatter(
        lax.dot_general(
            normalized, grad_kv, (((0,), (0,)), ((), ())), preferred_element_type=jnp.float32
        ),
        "dp",
        scatter_dimension=0,
        tiled=True,
    )
    new_first = 0.9 * first_moment + 0.1 * weight_grad
    new_second = 0.999 * second_moment + 0.001 * weight_grad * weight_grad
    first_hat = new_first / bias_first
    second_hat = new_second / bias_second
    new_master = master - 0.01 * (first_hat / (jnp.sqrt(second_hat) + 1e-08) + 0.1 * master)
    new_replica = lax.all_gather(new_master.astype(jnp.bfloat16), "dp", axis=0, tiled=True)
    return (grad_hidden, new_master, new_first, new_second, new_replica)


def solution(mesh):
    placed = (
        P("dp", None),
        P(),
        P(None, "tensor"),
        P("tensor", None),
        P("dp", "tensor"),
        P("dp", "tensor"),
        P("dp", "tensor"),
        P("dp", "tensor"),
    )
    return jax.shard_map(
        local,
        mesh=mesh,
        in_specs=placed,
        out_specs=(
            P("dp", "tensor"),
            P("dp", "tensor"),
            P("dp", "tensor"),
            P("dp", "tensor"),
            P(None, "tensor"),
        ),
        check_vma=False,
    )
```

profile of v0, /device:TPU:1, one launch (start us, length us, event | category | flops | bytes accessed | tf_op | source)
XLA Modules:
  0.0 142.4 jit_solution(14229155059456331807)
XLA Ops:
  8.0 0.0 copy-start
  8.0 0.0 reduce-scatter.2.cloned.1.call-start
  8.1 1.4 fusion.8
  9.4 0.3 copy-done
  9.8 4.4 %fusion.9 = f32[512,2048]{1,0:T(8,128)} fusion(bf16[512,2048]{1,0:T(8,128)(2,1)S(1)} %copy-done, bf16[512,512]{1,0:T(8,128)(2,1)} %param.8, f32[512]{0:T(512)} %param.9, f32[512]{0:T(512)S(1)} %add_rsqrt_fusion), kind=kOutput, calls=%fused_computation.12 | convolution fusion | flops 1074790400 | bytes 6819840 | tf_op jit(solution)/shard_map/dot_general | solution.py:34
  14.1 0.0 reduce-scatter.2.cloned.1.call-update
  14.1 0.0 copy-start.2
  14.2 0.0 copy-start.3
  14.2 0.0 copy-start.4
  14.2 0.0 all-reduce.2.cloned.1.call-start
  14.2 3.9 %fusion.20 = f32[512,512]{1,0:T(8,128)} fusion(bf16[512,2048]{1,0:T(8,128)(2,1)S(1)} %copy-done, bf16[512,2048]{1,0:T(8,128)(2,1)} %param.10), kind=kOutput, calls=%fused_computation.25 | convolution fusion | flops 1073741824 | bytes 5242880 | tf_op jit(solution)/shard_map/dot_general | solution.py:25
  18.1 0.0 copy-start.1
  18.1 0.0 copy-start.5
  18.1 0.0 all-reduce.2.cloned.1.call-update
  18.2 0.0 all-gather.2.cloned.1.call-start
  18.2 68.8 %reduce-scatter.2.cloned.1.call-done = f32[32,2048]{1,0:T(8,128)} async-done(((f32[512,2048]{1,0:T(8,128)}), f32[32,2048]{1,0:T(8,128)}) %reduce-scatter.2.cloned.1.call-update) | async-done | bytes 262160 | tf_op jit(solution)/shard_map/reduce_scatter | solution.py:33
  87.0 0.0 copy-done.2
  87.0 0.0 copy-done.3
  87.0 0.0 copy-done.4
  87.0 2.0 %fusion.18 = (bf16[32,2048]{1,0:T(8,128)(2,1)}, f32[32,2048]{1,0:T(8,128)}, f32[32,2048]{1,0:T(8,128)}, f32[32,2048]{1,0:T(8,128)}) fusion(f32[32,2048]{1,0:T(8,128)S(1)} %copy-done.2, f32[32,2048]{1,0:T(8,128)} %reduce-scatter.2.cloned.1.call-done, f32[32,2048]{1,0:T(8,128)S(1)} %copy-done.3, f32[32,2048]{1,0:T(8,128)S(1)} %copy-done.4), kind=kLoop, calls=%fused_computation.24 | loop fusion | flops 1048576 | bytes 1966080 | tf_op jit(solution)/shard_map/convert_element_type | solution.py:46
  89.0 0.0 all-gather.2.cloned.1.call-update
  89.1 0.0 all-reduce.2.cloned.1.call-done
  89.1 0.0 copy-done.1
  89.1 0.0 copy-done.5
  89.1 1.5 %fusion.3 = f32[512]{0:T(512)S(1)} fusion(bf16[512,512]{1,0:T(8,128)(2,1)S(1)} %copy-done.1, f32[512,512]{1,0:T(8,128)} %all-reduce.2.cloned.1.call-done, f32[512]{0:T(512)S(1)} %copy-done.5, f32[512]{0:T(512)S(1)} %add_rsqrt_fusion), kind=kLoop, calls=%fused_computation.6 | loop fusion | flops 1310208 | bytes 1579008 | tf_op jit(solution)/shard_map/reduce_sum | solution.py:15
  90.7 6.4 %convolution_convert_fusion = bf16[512,3584]{1,0:T(8,128)(2,1)} fusion(bf16[3584,512]{1,0:T(8,128)(2,1)} %param.11, bf16[512,512]{1,0:T(8,128)(2,1)S(1)} %copy-done.1, f32[512,512]{1,0:T(8,128)} %all-reduce.2.cloned.1.call-done, f32[512]{0:T(512)S(1)} %broadcast_multiply_fusion, f32[512]{0:T(512)S(1)} %copy-done.5, f32[512]{0:T(512)S(1)} %add_rsqrt_fusion), kind=kOutput, calls=%fused_computation | convolution fusion | flops 1882718208 | bytes 8919040 | tf_op jit(solution)/shard_map/dot_general | solution.py:30
  97.0 34.8 %all-gather.2.cloned.1.call-done = bf16[512,2048]{1,0:T(8,128)(2,1)} async-done(((bf16[32,2048]{1,0:T(8,128)(2,1)}), bf16[512,2048]{1,0:T(8,128)(2,1)}) %all-gather.2.cloned.1.call-update) | async-done | bytes 2097168 | tf_op jit(solution)/shard_map/all_gather | solution.py:46
  131.8 3.2 %copy.15 = bf16[512,2048]{1,0:T(8,128)(2,1)} copy(bf16[512,2048]{1,0:T(8,128)(2,1)} %all-gather.2.cloned.1.call-done) | data formatting | bytes 4194304
  (2 shorter events, 0.0 us)
Async XLA Ops:
  8.0 1.8 %copy-start = (bf16[512,2048]{1,0:T(8,128)(2,1)S(1)}, bf16[512,2048]{1,0:T(8,128)(2,1)}, u32[]{:S(2)}) copy-start(bf16[512,2048]{1,0:T(8,128)(2,1)} %param.12) | copy-start | bytes 6291460
  8.0 79.0 %reduce-scatter.2.cloned.1.call-start = ((), (), s32[]{:S(2)}) async-start(), calls=%async_computation.2 | async-start | bytes 4456448 | tf_op jit(solution)/shard_map/reduce_scatter | solution.py:33
  14.1 72.9 %copy-start.2 = (f32[32,2048]{1,0:T(8,128)S(1)}, f32[32,2048]{1,0:T(8,128)}, u32[]{:S(2)}) copy-start(f32[32,2048]{1,0:T(8,128)} %param.13) | copy-start | bytes 786436
  14.2 72.9 %copy-start.3 = (f32[32,2048]{1,0:T(8,128)S(1)}, f32[32,2048]{1,0:T(8,128)}, u32[]{:S(2)}) copy-start(f32[32,2048]{1,0:T(8,128)} %param.14) | copy-start | bytes 786436
  14.2 72.9 %copy-start.4 = (f32[32,2048]{1,0:T(8,128)S(1)}, f32[32,2048]{1,0:T(8,128)}, u32[]{:S(2)}) copy-start(f32[32,2048]{1,0:T(8,128)} %param.15) | copy-start | bytes 786436
  14.2 74.9 %all-reduce.2.cloned.1.call-start = ((), (), s32[]{:S(2)}) async-start(), calls=%async_computation.1 | async-start | bytes 2097152 | tf_op jit(solution)/shard_map/psum | solution.py:28
  18.1 71.0 %copy-start.1 = (bf16[512,512]{1,0:T(8,128)(2,1)S(1)}, bf16[512,512]{1,0:T(8,128)(2,1)}, u32[]{:S(2)}) copy-start(bf16[512,512]{1,0:T(8,128)(2,1)} %param.8) | copy-start | bytes 1572868
  18.1 71.0 %copy-start.5 = (f32[512]{0:T(512)S(1)}, f32[512]{0:T(512)}, u32[]{:S(2)}) copy-start(f32[512]{0:T(512)} %param.9) | copy-start | bytes 6148
  18.2 113.7 %all-gather.2.cloned.1.call-start = ((), (), s32[]{:S(2)}) async-start(), calls=%async_computation.3 | async-start | bytes 2228224 | tf_op jit(solution)/shard_map/all_gather | solution.py:46
Sparse Core Ops, SparseCore 0:
  14.3 72.7 reduce-scatter.1
  89.2 42.5 all-gather.1
Sparse Core Ops, SparseCore 1:
  18.2 41.8 all-reduce.1
where the time goes:
time: 143 us; the launch traced here: 142 us
  waiting for transfers between devices  104 us (73%)
  between operations  15.5 us (11%)
  matrix products  14.6 us (10%)
  other arithmetic  4.91 us (3%)
  local copies, waits for them, and re-layouts  3.51 us (2%)
    reduce_scatter x1, waiting for transfers between devices, local(): lax.psum_scatter(lax.dot_general(normalized, grad_kv, (((0,), (0,)), ((),...  68.8 us
    all_gather x1, waiting for transfers between devices, local(): lax.all_gather(new_master.astype(jnp.bfloat16), 'dp', axis=0, tiled=True)  34.8 us
    dot_general x1, matrix products, local(): lax.dot_general(grad_pre, down_weight, (((1,), (1,)), ((), ())), preferre...  6.38 us
    dot_general x1, matrix products, local(): lax.dot_general(normalized, grad_kv, (((0,), (0,)), ((), ())), preferred_...  4.37 us
    dot_general x1, matrix products, local(): lax.dot_general(grad_kv, kv_weight, (((1,), (1,)), ((), ())), preferred_e...  3.9 us
    unnamed x13, local copies, waits for them, and re-layouts  3.51 us
  transfers between devices with their start and end apart: 3, of which 2 were waited for; matrix products, arithmetic and copies ran while one was open for 10% of the time, Pallas kernels for 0%

commit v1 on v0

v1 whole, which is shorter than its diff:
```python
import functools

import jax
import jax.numpy as jnp
from jax import lax
from jax.experimental import pallas as pl
from jax.experimental.pallas import tpu as pltpu
from jax.sharding import PartitionSpec as P

bias_first = 0.9999734386011124
bias_second = 0.09520785288629112
MESH = pl.DeviceIdType.MESH


def norm_backward(latent_rows, norm_gain, grad_rows):
    values = latent_rows.astype(jnp.float32)
    inverse_rms = lax.rsqrt(jnp.mean(values * values, axis=1, keepdims=True) + 1e-06)
    unit = values * inverse_rms
    scaled = grad_rows * norm_gain
    inner = jnp.mean(scaled * unit, axis=1, keepdims=True)
    return (inverse_rms * (scaled - unit * inner)).astype(jnp.bfloat16)


def normalize(latent_pre, norm_gain):
    values = latent_pre.astype(jnp.float32)
    inverse_rms = lax.rsqrt(jnp.mean(values * values, axis=1, keepdims=True) + 1e-06)
    return values * inverse_rms * norm_gain


def adamw(master, first_moment, second_moment, weight_grad):
    new_first = 0.9 * first_moment + 0.1 * weight_grad
    new_second = 0.999 * second_moment + 0.001 * weight_grad * weight_grad
    first_hat = new_first / bias_first
    second_hat = new_second / bias_second
    new_master = master - 0.01 * (first_hat / (jnp.sqrt(second_hat) + 1e-08) + 0.1 * master)
    return new_master, new_first, new_second


def project(grad_pre, down_weight):
    return lax.dot_general(
        grad_pre, down_weight, (((1,), (1,)), ((), ())), preferred_element_type=jnp.float32
    ).astype(jnp.bfloat16)


def local_small_rows(
    latent_pre, norm_gain, kv_weight, down_weight, grad_kv, master, first_moment, second_moment
):
    normalized = normalize(latent_pre, norm_gain).astype(jnp.bfloat16)
    partial_grad = lax.dot_general(
        grad_kv, kv_weight, (((1,), (1,)), ((), ())), preferred_element_type=jnp.float32
    )
    grad_latent = lax.psum(partial_grad, "tensor")
    grad_hidden = project(norm_backward(latent_pre, norm_gain, grad_latent), down_weight)
    weight_grad = lax.psum_scatter(
        lax.dot_general(
            normalized, grad_kv, (((0,), (0,)), ((), ())), preferred_element_type=jnp.float32
        ),
        "dp",
        scatter_dimension=0,
        tiled=True,
    )
    new_master, new_first, new_second = adamw(master, first_moment, second_moment, weight_grad)
    new_replica = lax.all_gather(new_master.astype(jnp.bfloat16), "dp", axis=0, tiled=True)
    return (grad_hidden, new_master, new_first, new_second, new_replica)


def kernel(
    Z, T, K,
    latent, gain, kvw, gkv, master, first, second,
    gp, new_master, new_first, new_second, rep,
    norm_t, acc, core_in, x_out, x_in, z_out, z_in, lat_out, lat_in, lat_own,
    core_s, core_r, x_s, x_r, z_s, z_r, lat_s, lat_r, gp_s, gp_r,
    agz_s, agz_r, agx_s, agx_r, agc_s, agc_r,
):
    me = lax.axis_index("dp")
    t = lax.axis_index("tensor")
    z, x, c = me // 4, (me // 2) % 2, me % 2
    rows, W = acc.shape[-2], acc.shape[-1]
    half = lat_own.shape[0]

    def at(zz, xx, cc):
        return zz * 4 + xx * 2 + cc

    core_peer = {"dp": at(z, x, 1 - c)}
    x_peer = {"dp": at(z, 1 - x, c)}
    z_to = [None] + [lax.rem(z + d, Z) for d in range(1, Z)]
    z_from = [z] + [lax.rem(z - d + Z, Z) for d in range(1, Z)]
    t_to = [None] + [lax.rem(t + d, T) for d in range(1, T)]

    barrier = pltpu.get_barrier_semaphore()
    peers = [core_peer, x_peer]
    peers += [{"dp": at(z_to[d], x, c)} for d in range(1, Z)]
    peers += [{"tensor": t_to[d]} for d in range(1, T)]
    for peer in peers:
        pl.semaphore_signal(barrier, inc=1, device_id=peer, device_id_type=MESH)

    started = []

    def send(src, dst, s, r, peer):
        copy = pltpu.make_async_remote_copy(
            src_ref=src, dst_ref=dst, send_sem=s, recv_sem=r, device_id=peer, device_id_type=MESH
        )
        copy.start()
        started.append(copy)
        return copy

    norm_t[...] = jnp.transpose(normalize(latent[...], gain[...])).astype(jnp.bfloat16)

    def weight_chunk(k):
        part = jnp.dot(
            norm_t[...], gkv[:, k * W:(k + 1) * W], preferred_element_type=jnp.float32
        )
        acc[k] = part.reshape(Z, 2, 2, rows, W)

    def send_core(k):
        return send(
            acc.at[k, :, :, 1 - c], core_in.at[k], core_s.at[k], core_r.at[k], core_peer
        )

    def latent_part(index):
        start = pl.multiple_of(index * half, half)
        return lax.dot_general(
            gkv[pl.ds(start, half), :], kvw[...], (((1,), (1,)), ((), ())),
            preferred_element_type=jnp.float32,
        )

    weight_chunk(0)
    pl.semaphore_wait(barrier, len(peers))
    core = [send_core(0)]
    lat = [None]
    for d in range(1, T):
        lat_out[d - 1] = latent_part(t_to[d])
        lat.append(send(
            lat_out.at[d - 1], lat_in.at[d - 1], lat_s.at[d - 1], lat_r.at[d - 1],
            {"tensor": t_to[d]},
        ))
    xs = []

    def stage_x(k):
        core[k].wait_recv()
        x_out[k] = (acc[k, :, 1 - x, c] + core_in[k, :, 1 - x]).astype(jnp.bfloat16)
        xs.append(send(x_out.at[k], x_in.at[k], x_s.at[k], x_r.at[k], x_peer))

    for k in range(1, K):
        weight_chunk(k)
        core.append(send_core(k))
        stage_x(k - 1)
    stage_x(K - 1)
    lat_own[...] = latent_part(t)

    def block_sum(k, zz):
        return acc[k, zz, x, c] + core_in[k, zz, x] + x_in[k, zz].astype(jnp.float32)

    zs = []
    for k in range(K):
        xs[k].wait_recv()
        zs.append([])
        for d in range(1, Z):
            z_out[k, d - 1] = block_sum(k, z_to[d]).astype(jnp.bfloat16)
            zs[k].append(send(
                z_out.at[k, d - 1], z_in.at[k, d - 1], z_s.at[k, d - 1], z_r.at[k, d - 1],
                {"dp": at(z_to[d], x, c)},
            ))

    def gather(zz, xx, cc, k, s, r, peer):
        block = rep.at[at(zz, xx, cc), :, pl.ds(k * W, W)]
        return send(block, block, s, r, peer)

    agz, agx, agc = [], [], []

    def update(k):
        for copy in zs[k]:
            copy.wait_recv()
        total = block_sum(k, z)
        for d in range(1, Z):
            total = total + z_in[k, d - 1].astype(jnp.float32)
        cols = slice(k * W, (k + 1) * W)
        fresh, new_first[:, cols], new_second[:, cols] = adamw(
            master[:, cols], first[:, cols], second[:, cols], total
        )
        new_master[:, cols] = fresh
        rep[me, :, cols] = fresh.astype(jnp.bfloat16)
        agz.append([
            gather(z, x, c, k, agz_s.at[k, d - 1], agz_r.at[k, d - 1], {"dp": at(z_to[d], x, c)})
            for d in range(1, Z)
        ])
        agx.append([gather(z, x, c, k, agx_s.at[k, 0], agx_r.at[k, 0], x_peer)])
        agc.append([gather(z, x, c, k, agc_s.at[k, 0], agc_r.at[k, 0], core_peer)])

    def forward(k):
        for d in range(1, Z):
            agz[k][d - 1].wait_recv()
            agx[k].append(
                gather(z_from[d], x, c, k, agx_s.at[k, d], agx_r.at[k, d], x_peer)
            )
            agc[k].append(
                gather(z_from[d], x, c, k, agc_s.at[k, d], agc_r.at[k, d], core_peer)
            )

    def forward_core(k):
        for d in range(Z):
            agx[k][d].wait_recv()
            agc[k].append(gather(
                z_from[d], 1 - x, c, k, agc_s.at[k, Z + d], agc_r.at[k, Z + d], core_peer
            ))

    update(0)
    grad = lat_own[...]
    for d in range(1, T):
        lat[d].wait_recv()
        grad = grad + lat_in[d - 1]
    gp[t] = norm_backward(latent[pl.ds(pl.multiple_of(t * half, half), half), :], gain[...], grad)
    gps = [
        send(gp.at[t], gp.at[t], gp_s.at[d - 1], gp_r.at[d - 1], {"tensor": t_to[d]})
        for d in range(1, T)
    ]
    for k in range(1, K):
        update(k)
        forward(k - 1)
        if k >= 2:
            forward_core(k - 2)
    forward(K - 1)
    for k in range(max(K - 2, 0), K):
        forward_core(k)
    for k in range(K):
        for copy in agc[k]:
            copy.wait_recv()
    for copy in gps:
        copy.wait_recv()
    for copy in started:
        copy.wait_send()


def local(
    Z, T,
    latent_pre, norm_gain, kv_weight, down_weight, grad_kv, master, first_moment, second_moment,
):
    tokens, width = latent_pre.shape
    rows, columns = master.shape
    dp, half, K = 4 * Z, tokens // T, 4
    W = columns // K
    f32, bf16, DMA = jnp.float32, jnp.bfloat16, pltpu.SemaphoreType.DMA
    state = jax.ShapeDtypeStruct((rows, columns), f32)
    vmem = pl.BlockSpec(memory_space=pltpu.VMEM)
    grad_pre, new_master, new_first, new_second, replica = pl.pallas_call(
        functools.partial(kernel, Z, T, K),
        out_shape=(
            jax.ShapeDtypeStruct((T, half, width), bf16),
            state, state, state,
            jax.ShapeDtypeStruct((dp, rows, columns), bf16),
        ),
        in_specs=[vmem] * 7,
        out_specs=(vmem,) * 5,
        scratch_shapes=[
            pltpu.VMEM((width, tokens), bf16),
            pltpu.VMEM((K, Z, 2, 2, rows, W), f32),
            pltpu.VMEM((K, Z, 2, rows, W), f32),
            pltpu.VMEM((K, Z, rows, W), bf16),
            pltpu.VMEM((K, Z, rows, W), bf16),
            pltpu.VMEM((K, Z - 1, rows, W), bf16),
            pltpu.VMEM((K, Z - 1, rows, W), bf16),
            pltpu.VMEM((T - 1, half, width), f32),
            pltpu.VMEM((T - 1, half, width), f32),
            pltpu.VMEM((half, width), f32),
            DMA((K,)), DMA((K,)), DMA((K,)), DMA((K,)),
            DMA((K, Z - 1)), DMA((K, Z - 1)),
            DMA((T - 1,)), DMA((T - 1,)), DMA((T - 1,)), DMA((T - 1,)),
            DMA((K, Z - 1)), DMA((K, Z - 1)),
            DMA((K, Z)), DMA((K, Z)),
            DMA((K, 2 * Z)), DMA((K, 2 * Z)),
        ],
        compiler_params=pltpu.CompilerParams(
            collective_id=0, has_side_effects=True, vmem_limit_bytes=40 * 1024 * 1024
        ),
    )(latent_pre, norm_gain.reshape(1, width), kv_weight, grad_kv, master, first_moment, second_moment)
    grad_hidden = project(grad_pre.reshape(tokens, width), down_weight)
    return (grad_hidden, new_master, new_first, new_second, replica.reshape(dp * rows, columns))


def solution(mesh):
    dp, T = mesh.shape["dp"], mesh.shape["tensor"]

    def body(*args):
        rows = args[5].shape[0]
        if dp % 4 == 0 and dp > 4 and T > 1 and rows % 16 == 0:
            return local(dp // 4, T, *args)
        return local_small_rows(*args)

    placed = (
        P("dp", None),
        P(),
        P(None, "tensor"),
        P("tensor", None),
        P("dp", "tensor"),
        P("dp", "tensor"),
        P("dp", "tensor"),
        P("dp", "tensor"),
    )
    return jax.shard_map(
        body,
        mesh=mesh,
        in_specs=placed,
        out_specs=(
            P("dp", "tensor"),
            P("dp", "tensor"),
            P("dp", "tensor"),
            P("dp", "tensor"),
            P(None, "tensor"),
        ),
        check_vma=False,
    )
```

time: 143 us -> 59.1 us (0.41)
  waiting for transfers between devices: 104 us -> 0 us
  Pallas kernels: 0 us -> 43 us
  between operations: 15.5 us -> 0.67 us
  matrix products: 14.6 us -> 3.94 us
  local copies, waits for them, and re-layouts: 3.51 us -> 11.2 us
  other arithmetic: 4.91 us -> 0 us
    reduce_scatter x1 -> x0, waiting for transfers between devices: 68.8 us -> none  [local(): lax.psum_scatter(lax.dot_general(normalized, grad_kv, (((0,), (0,)), ((),...]
    pallas_call x0 -> x1, Pallas kernels: none -> 43 us  [local(): pl.pallas_call(functools.partial(kernel, Z, T, K), out_shape=(jax.ShapeDt...]
    all_gather x1 -> x0, waiting for transfers between devices: 34.8 us -> none  [local(): lax.all_gather(new_master.astype(jnp.bfloat16), 'dp', axis=0, tiled=True)]
    dot_general x3 -> x1, matrix products: 14.6 us -> 3.94 us  [project(): lax.dot_general(grad_pre, down_weight, (((1,), (1,)), ((), ())), preferre...]
    unnamed x13 -> x20, local copies, waits for them, and re-layouts: 3.51 us -> 11.2 us
    reduce_sum x2 -> x0, other arithmetic: 2.9 us -> none  [the longest x1 1.54 us: norm_backward(): inner = jnp.mean(scaled * unit, axis=1, keepdims=True)]
    convert_element_type x1 -> x0, other arithmetic: 2 us -> none  [local(): new_master.astype(jnp.bfloat16)]
  transfers between devices with their start and end apart: 3 -> 0, of which waited for: 2 -> 0; matrix products, arithmetic and copies ran while one was open for 10% -> 0% of each run, Pallas kernels for 0% -> 0%
where the time goes in v1:
time: 59.1 us; the launch traced here: 58.8 us
  Pallas kernels  43 us (73%)
  local copies, waits for them, and re-layouts  11.2 us (19%)
  matrix products  3.94 us (7%)
  between operations  0.67 us (1%)
    pallas_call x1, Pallas kernels, local(): pl.pallas_call(functools.partial(kernel, Z, T, K), out_shape=(jax.ShapeDt...  43 us
    unnamed x20, local copies, waits for them, and re-layouts  11.2 us
    dot_general x1, matrix products, project(): lax.dot_general(grad_pre, down_weight, (((1,), (1,)), ((), ())), preferre...  3.94 us

profile of v1, /device:TPU:1, one launch (start us, length us, event | category | flops | bytes accessed | tf_op | source)
XLA Modules:
  0.0 58.8 jit_solution(17122556137604714899)
XLA Ops:
  0.6 0.0 copy-start
  0.6 1.6 %copy-done = bf16[512,2048]{1,0:T(8,128)(2,1)S(1)} copy-done((bf16[512,2048]{1,0:T(8,128)(2,1)S(1)}, bf16[512,2048]{1,0:T(8,128)(2,1)}, u32[]{:S(2)}) %copy-start) | copy-done | bytes 2097176
  2.2 0.0 copy-start.1
  2.2 1.6 %copy-done.1 = bf16[512,2048]{1,0:T(8,128)(2,1)S(1)} copy-done((bf16[512,2048]{1,0:T(8,128)(2,1)S(1)}, bf16[512,2048]{1,0:T(8,128)(2,1)}, u32[]{:S(2)}) %copy-start.1) | copy-done | bytes 2097176
  3.8 0.0 copy-start.2
  3.8 1.0 %copy-done.2 = bf16[512,512]{1,0:T(8,128)(2,1)S(1)} copy-done((bf16[512,512]{1,0:T(8,128)(2,1)S(1)}, bf16[512,512]{1,0:T(8,128)(2,1)}, u32[]{:S(2)}) %copy-start.2) | copy-done | bytes 524312
  4.9 0.0 copy-start.3
  4.9 0.9 %copy-done.3 = f32[32,2048]{1,0:T(8,128)S(1)} copy-done((f32[32,2048]{1,0:T(8,128)S(1)}, f32[32,2048]{1,0:T(8,128)}, u32[]{:S(2)}) %copy-start.3) | copy-done | bytes 262168
  5.8 0.0 copy-start.4
  5.8 0.9 %copy-done.4 = f32[32,2048]{1,0:T(8,128)S(1)} copy-done((f32[32,2048]{1,0:T(8,128)S(1)}, f32[32,2048]{1,0:T(8,128)}, u32[]{:S(2)}) %copy-start.4) | copy-done | bytes 262168
  6.8 0.0 copy-start.5
  6.8 0.9 %copy-done.5 = f32[32,2048]{1,0:T(8,128)S(1)} copy-done((f32[32,2048]{1,0:T(8,128)S(1)}, f32[32,2048]{1,0:T(8,128)}, u32[]{:S(2)}) %copy-start.5) | copy-done | bytes 262168
  7.7 0.0 copy-start.6
  7.7 0.7 %copy-done.6 = f32[512]{0:T(512)S(1)} copy-done((f32[512]{0:T(512)S(1)}, f32[512]{0:T(512)}, u32[]{:S(2)}) %copy-start.6) | copy-done | bytes 2072
  8.4 0.0 copy-start.7
  8.4 43.0 %shard_map.119 = (bf16[2,256,512]{2,1,0:T(8,128)(2,1)S(1)}, f32[32,2048]{1,0:T(8,128)S(1)}, f32[32,2048]{1,0:T(8,128)S(1)}, f32[32,2048]{1,0:T(8,128)S(1)}, bf16[16,32,2048]{2,1,0:T(8,128)(2,1)S(1)}) custom-call(bf16[512,512]{1,0:T(8,128)(2,1)S(1)} %copy-done.2, f32[1,512]{1,0:T(1,128)S(1)} %bitcast.6, bf16[512,2048]{1,0:T(8,128)(2,1)S(1)} %copy-done, ...), custom_call_target="tpu_custom_call" | custom-call | tf_op jit(solution)/shard_map/pallas_call | solution.py:245
  51.4 0.0 copy-done.7
  51.4 3.9 %convolution_convert_fusion = bf16[512,3584]{1,0:T(8,128)(2,1)} fusion(bf16[512,512]{1,0:T(8,128)(2,1)S(1)} %bitcast.7, bf16[3584,512]{1,0:T(8,128)(2,1)S(1)} %copy-done.7), kind=kOutput, calls=%fused_computation | convolution fusion | flops 1880883200 | bytes 7864320 | tf_op jit(solution)/shard_map/dot_general | solution.py:40
  55.4 0.7 %copy.17 = f32[32,2048]{1,0:T(8,128)} copy(f32[32,2048]{1,0:T(8,128)S(1)} %get-tuple-element.21) | data formatting | bytes 524288
  56.1 0.7 %copy.18 = f32[32,2048]{1,0:T(8,128)} copy(f32[32,2048]{1,0:T(8,128)S(1)} %get-tuple-element.22) | data formatting | bytes 524288
  56.8 0.7 %copy.19 = f32[32,2048]{1,0:T(8,128)} copy(f32[32,2048]{1,0:T(8,128)S(1)} %get-tuple-element.23) | data formatting | bytes 524288
  57.5 1.3 %copy.20 = bf16[512,2048]{1,0:T(8,128)(2,1)} copy(bf16[512,2048]{1,0:T(8,128)(2,1)S(1)} %bitcast.5) | data formatting | bytes 4194304
Async XLA Ops:
  0.6 1.6 %copy-start = (bf16[512,2048]{1,0:T(8,128)(2,1)S(1)}, bf16[512,2048]{1,0:T(8,128)(2,1)}, u32[]{:S(2)}) copy-start(bf16[512,2048]{1,0:T(8,128)(2,1)} %kvw.1) | copy-start | bytes 6291460
  2.2 1.6 %copy-start.1 = (bf16[512,2048]{1,0:T(8,128)(2,1)S(1)}, bf16[512,2048]{1,0:T(8,128)(2,1)}, u32[]{:S(2)}) copy-start(bf16[512,2048]{1,0:T(8,128)(2,1)} %gkv.1) | copy-start | bytes 6291460
  3.8 1.0 %copy-start.2 = (bf16[512,512]{1,0:T(8,128)(2,1)S(1)}, bf16[512,512]{1,0:T(8,128)(2,1)}, u32[]{:S(2)}) copy-start(bf16[512,512]{1,0:T(8,128)(2,1)} %latent.1) | copy-start | bytes 1572868
  4.9 0.9 %copy-start.3 = (f32[32,2048]{1,0:T(8,128)S(1)}, f32[32,2048]{1,0:T(8,128)}, u32[]{:S(2)}) copy-start(f32[32,2048]{1,0:T(8,128)} %master.1) | copy-start | bytes 786436
  5.8 0.9 %copy-start.4 = (f32[32,2048]{1,0:T(8,128)S(1)}, f32[32,2048]{1,0:T(8,128)}, u32[]{:S(2)}) copy-start(f32[32,2048]{1,0:T(8,128)} %first.1) | copy-start | bytes 786436
  6.8 0.9 %copy-start.5 = (f32[32,2048]{1,0:T(8,128)S(1)}, f32[32,2048]{1,0:T(8,128)}, u32[]{:S(2)}) copy-start(f32[32,2048]{1,0:T(8,128)} %second.1) | copy-start | bytes 786436
  7.7 0.7 %copy-start.6 = (f32[512]{0:T(512)S(1)}, f32[512]{0:T(512)}, u32[]{:S(2)}) copy-start(f32[512]{0:T(512)} %param.9) | copy-start | bytes 6148
  8.4 43.0 %copy-start.7 = (bf16[3584,512]{1,0:T(8,128)(2,1)S(1)}, bf16[3584,512]{1,0:T(8,128)(2,1)}, u32[]{:S(2)}) copy-start(bf16[3584,512]{1,0:T(8,128)(2,1)} %param.11) | copy-start | bytes 11010052

commit v2 on v1

--- a/solution.py
+++ b/solution.py
@@ -66,16 +66,31 @@
 
 def kernel(
     Z, T, K,
-    latent, gain, kvw, gkv, master, first, second,
+    latent_h, gain_h, kvw_h, gkv_h, master_h, first_h, second_h,
     gp, new_master, new_first, new_second, rep,
+    latent, gain, kvw, gkv, master, first, second, load_s, gkv_s,
     norm_t, acc, core_in, x_out, x_in, z_out, z_in, lat_out, lat_in, lat_own,
     core_s, core_r, x_s, x_r, z_s, z_r, lat_s, lat_r, gp_s, gp_r,
     agz_s, agz_r, agx_s, agx_r, agc_s, agc_r,
 ):
+    rows, W = acc.shape[-2], acc.shape[-1]
+    pairs = (
+        (latent_h, latent), (gain_h, gain), (kvw_h, kvw),
+        (master_h, master), (first_h, first), (second_h, second),
+    )
+    loads = [pltpu.make_async_copy(a, b, load_s.at[i]) for i, (a, b) in enumerate(pairs)]
+    gkv_loads = [
+        pltpu.make_async_copy(
+            gkv_h.at[:, pl.ds(k * W, W)], gkv.at[:, pl.ds(k * W, W)], gkv_s.at[k]
+        )
+        for k in range(K)
+    ]
+    for copy in loads[:2] + gkv_loads + loads[2:]:
+        copy.start()
+
     me = lax.axis_index("dp")
     t = lax.axis_index("tensor")
     z, x, c = me // 4, (me // 2) % 2, me % 2
-    rows, W = acc.shape[-2], acc.shape[-1]
     half = lat_own.shape[0]
 
     def at(zz, xx, cc):
@@ -104,6 +119,8 @@
         started.append(copy)
         return copy
 
+    loads[0].wait()
+    loads[1].wait()
     norm_t[...] = jnp.transpose(normalize(latent[...], gain[...])).astype(jnp.bfloat16)
 
     def weight_chunk(k):
@@ -124,9 +141,13 @@
             preferred_element_type=jnp.float32,
         )
 
+    gkv_loads[0].wait()
     weight_chunk(0)
     pl.semaphore_wait(barrier, len(peers))
     core = [send_core(0)]
+    for copy in gkv_loads[1:]:
+        copy.wait()
+    loads[2].wait()
     lat = [None]
     for d in range(1, T):
         lat_out[d - 1] = latent_part(t_to[d])
@@ -204,6 +225,8 @@
                 z_from[d], 1 - x, c, k, agc_s.at[k, Z + d], agc_r.at[k, Z + d], core_peer
             ))
 
+    for copy in loads[3:]:
+        copy.wait()
     update(0)
     grad = lat_own[...]
     for d in range(1, T):
@@ -231,6 +254,36 @@
         copy.wait_send()
 
 
+def finish(
+    gp_h, down_h, master, first, second, rep,
+    hidden_h, master_h, first_h, second_h, rep_h,
+    gp, gp_s, down, down_s, tiles, out_s, tile_s,
+):
+    count, _, tile = tiles.shape
+    load = pltpu.make_async_copy(gp_h, gp, gp_s)
+    load.start()
+    down_loads = [
+        pltpu.make_async_copy(down_h.at[pl.ds(n * tile, tile), :], down.at[n], down_s.at[n])
+        for n in range(count)
+    ]
+    for copy in down_loads:
+        copy.start()
+    pairs = ((rep, rep_h), (master, master_h), (first, first_h), (second, second_h))
+    copies = [pltpu.make_async_copy(a, b, out_s.at[i]) for i, (a, b) in enumerate(pairs)]
+    for copy in copies:
+        copy.start()
+    load.wait()
+    for n in range(count):
+        down_loads[n].wait()
+        tiles[n] = project(gp[...], down[n])
+        copies.append(pltpu.make_async_copy(
+            tiles.at[n], hidden_h.at[:, pl.ds(n * tile, tile)], tile_s.at[n]
+        ))
+        copies[-1].start()
+    for copy in copies:
+        copy.wait()
+
+
 def local(
     Z, T,
     latent_pre, norm_gain, kv_weight, down_weight, grad_kv, master, first_moment, second_moment,
@@ -249,9 +302,17 @@
             state, state, state,
             jax.ShapeDtypeStruct((dp, rows, columns), bf16),
         ),
-        in_specs=[vmem] * 7,
+        in_specs=[pl.BlockSpec(memory_space=pltpu.HBM)] * 7,
         out_specs=(vmem,) * 5,
         scratch_shapes=[
+            pltpu.VMEM((tokens, width), bf16),
+            pltpu.VMEM((1, width), f32),
+            pltpu.VMEM((width, columns), bf16),
+            pltpu.VMEM((tokens, columns), bf16),
+            pltpu.VMEM((rows, columns), f32),
+            pltpu.VMEM((rows, columns), f32),
+            pltpu.VMEM((rows, columns), f32),
+            DMA((6,)), DMA((K,)),
             pltpu.VMEM((width, tokens), bf16),
             pltpu.VMEM((K, Z, 2, 2, rows, W), f32),
             pltpu.VMEM((K, Z, 2, rows, W), f32),
@@ -270,11 +331,32 @@
             DMA((K, 2 * Z)), DMA((K, 2 * Z)),
         ],
         compiler_params=pltpu.CompilerParams(
-            collective_id=0, has_side_effects=True, vmem_limit_bytes=40 * 1024 * 1024
+            collective_id=0, has_side_effects=True, vmem_limit_bytes=58 * 1024 * 1024
         ),
     )(latent_pre, norm_gain.reshape(1, width), kv_weight, grad_kv, master, first_moment, second_moment)
-    grad_hidden = project(grad_pre.reshape(tokens, width), down_weight)
-    return (grad_hidden, new_master, new_first, new_second, replica.reshape(dp * rows, columns))
+    model = down_weight.shape[0]
+    tile = next(n for n in (512, 256, 128, model) if model % n == 0)
+    any_space = pl.BlockSpec(memory_space=pltpu.HBM)
+    return pl.pallas_call(
+        finish,
+        out_shape=(
+            jax.ShapeDtypeStruct((tokens, model), bf16),
+            state, state, state,
+            jax.ShapeDtypeStruct((dp * rows, columns), bf16),
+        ),
+        in_specs=[any_space] * 6,
+        out_specs=(any_space,) * 5,
+        scratch_shapes=[
+            pltpu.VMEM((tokens, width), bf16), DMA,
+            pltpu.VMEM((model // tile, tile, width), bf16), DMA((model // tile,)),
+            pltpu.VMEM((model // tile, tokens, tile), bf16),
+            DMA((4,)), DMA((model // tile,)),
+        ],
+        compiler_params=pltpu.CompilerParams(vmem_limit_bytes=60 * 1024 * 1024),
+    )(
+        grad_pre.reshape(tokens, width), down_weight, new_master, new_first, new_second,
+        replica.reshape(dp * rows, columns),
+    )
 
 
 def solution(mesh):

time: 59.1 us -> 135 us (2.28)
  Pallas kernels: 43 us -> 134 us
  local copies, waits for them, and re-layouts: 11.2 us -> 0 us
  matrix products: 3.94 us -> 0 us
    pallas_call x0 -> x1, Pallas kernels: none -> 88.6 us  [local(): pl.pallas_call(finish, out_shape=(jax.ShapeDtypeStruct((tokens, model), b...]
    unnamed x20 -> x0, local copies, waits for them, and re-layouts: 11.2 us -> none
    dot_general x1 -> x0, matrix products: 3.94 us -> none  [project(): lax.dot_general(grad_pre, down_weight, (((1,), (1,)), ((), ())), preferre...]
    pallas_call x1, Pallas kernels: 43 us -> 45.1 us  [local(): pl.pallas_call(functools.partial(kernel, Z, T, K), out_shape=(jax.ShapeDt...]
where the time goes in v2:
time: 135 us; the launch traced here: 134 us
  Pallas kernels  134 us (99%)
    pallas_call x1, Pallas kernels, local(): pl.pallas_call(finish, out_shape=(jax.ShapeDtypeStruct((tokens, model), b...  88.6 us
    pallas_call x1, Pallas kernels, local(): pl.pallas_call(functools.partial(kernel, Z, T, K), out_shape=(jax.ShapeDt...  45.1 us

profile of v2, /device:TPU:1, one launch (start us, length us, event | category | flops | bytes accessed | tf_op | source)
XLA Modules:
  0.0 134.4 jit_solution(16688763043412835713)
XLA Ops:
  0.6 45.1 %shard_map.119 = (bf16[2,256,512]{2,1,0:T(8,128)(2,1)}, f32[32,2048]{1,0:T(8,128)}, f32[32,2048]{1,0:T(8,128)}, f32[32,2048]{1,0:T(8,128)}, bf16[16,32,2048]{2,1,0:T(8,128)(2,1)}) custom-call(bf16[512,512]{1,0:T(8,128)(2,1)} %latent_h.1, f32[1,512]{1,0:T(1,128)} %bitcast.5, bf16[512,2048]{1,0:T(8,128)(2,1)} %kvw_h.1, bf16[512,2048]{1,0:T(8,128)(2,1)} %gkv_h.1, ...), custom_call_target="tpu_custom_call" | custom-call | tf_op jit(solution)/shard_map/pallas_call | solution.py:298
  45.7 88.6 %shard_map.120 = (bf16[512,3584]{1,0:T(8,128)(2,1)}, f32[32,2048]{1,0:T(8,128)}, f32[32,2048]{1,0:T(8,128)}, f32[32,2048]{1,0:T(8,128)}, bf16[512,2048]{1,0:T(8,128)(2,1)}) custom-call(bf16[512,512]{1,0:T(8,128)(2,1)} %bitcast.4, bf16[3584,512]{1,0:T(8,128)(2,1)} %down_h.1, f32[32,2048]{1,0:T(8,128)} %get-tuple-element.11.master, ...), custom_call_target="tpu_custom_call" | custom-call | tf_op jit(solution)/shard_map/pallas_call | solution.py:340

commit v3 on v2

--- a/solution.py
+++ b/solution.py
@@ -258,6 +258,7 @@
     gp_h, down_h, master, first, second, rep,
     hidden_h, master_h, first_h, second_h, rep_h,
     gp, gp_s, down, down_s, tiles, out_s, tile_s,
+    rep_v, master_v, first_v, second_v, in_s,
 ):
     count, _, tile = tiles.shape
     load = pltpu.make_async_copy(gp_h, gp, gp_s)
@@ -268,10 +269,14 @@
     ]
     for copy in down_loads:
         copy.start()
-    pairs = ((rep, rep_h), (master, master_h), (first, first_h), (second, second_h))
-    copies = [pltpu.make_async_copy(a, b, out_s.at[i]) for i, (a, b) in enumerate(pairs)]
-    for copy in copies:
+    trips = (
+        (rep, rep_v, rep_h), (master, master_v, master_h),
+        (first, first_v, first_h), (second, second_v, second_h),
+    )
+    arrivals = [pltpu.make_async_copy(a, v, in_s.at[i]) for i, (a, v, _) in enumerate(trips)]
+    for copy in arrivals:
         copy.start()
+    copies = []
     load.wait()
     for n in range(count):
         down_loads[n].wait()
@@ -280,6 +285,11 @@
             tiles.at[n], hidden_h.at[:, pl.ds(n * tile, tile)], tile_s.at[n]
         ))
         copies[-1].start()
+        if n == 0:
+            for i, (_, v, b) in enumerate(trips):
+                arrivals[i].wait()
+                copies.append(pltpu.make_async_copy(v, b, out_s.at[i]))
+                copies[-1].start()
     for copy in copies:
         copy.wait()
 
@@ -351,6 +361,11 @@
             pltpu.VMEM((model // tile, tile, width), bf16), DMA((model // tile,)),
             pltpu.VMEM((model // tile, tokens, tile), bf16),
             DMA((4,)), DMA((model // tile,)),
+            pltpu.VMEM((dp * rows, columns), bf16),
+            pltpu.VMEM((rows, columns), f32),
+            pltpu.VMEM((rows, columns), f32),
+            pltpu.VMEM((rows, columns), f32),
+            DMA((4,)),
         ],
         compiler_params=pltpu.CompilerParams(vmem_limit_bytes=60 * 1024 * 1024),
     )(

time: 135 us -> 53 us (0.39)
  Pallas kernels: 134 us -> 52.2 us
    pallas_call x1, Pallas kernels: 88.6 us -> 7.08 us  [local(): pl.pallas_call(finish, out_shape=(jax.ShapeDtypeStruct((tokens, model), b...]
where the time goes in v3:
time: 53 us; the launch traced here: 52.8 us
  Pallas kernels  52.2 us (98%)
  between operations  0.64 us (1%)
    pallas_call x1, Pallas kernels, local(): pl.pallas_call(functools.partial(kernel, Z, T, K), out_shape=(jax.ShapeDt...  45.1 us
    pallas_call x1, Pallas kernels, local(): pl.pallas_call(finish, out_shape=(jax.ShapeDtypeStruct((tokens, model), b...  7.08 us

profile of v3, /device:TPU:1, one launch (start us, length us, event | category | flops | bytes accessed | tf_op | source)
XLA Modules:
  0.0 52.8 jit_solution(18374525532457090886)
XLA Ops:
  0.6 45.1 %shard_map.119 = (bf16[2,256,512]{2,1,0:T(8,128)(2,1)}, f32[32,2048]{1,0:T(8,128)}, f32[32,2048]{1,0:T(8,128)}, f32[32,2048]{1,0:T(8,128)}, bf16[16,32,2048]{2,1,0:T(8,128)(2,1)}) custom-call(bf16[512,512]{1,0:T(8,128)(2,1)} %latent_h.1, f32[1,512]{1,0:T(1,128)} %bitcast.5, bf16[512,2048]{1,0:T(8,128)(2,1)} %kvw_h.1, bf16[512,2048]{1,0:T(8,128)(2,1)} %gkv_h.1, ...), custom_call_target="tpu_custom_call" | custom-call | tf_op jit(solution)/shard_map/pallas_call | solution.py:308
  45.7 7.1 %shard_map.120 = (bf16[512,3584]{1,0:T(8,128)(2,1)}, f32[32,2048]{1,0:T(8,128)}, f32[32,2048]{1,0:T(8,128)}, f32[32,2048]{1,0:T(8,128)}, bf16[512,2048]{1,0:T(8,128)(2,1)}) custom-call(bf16[512,512]{1,0:T(8,128)(2,1)} %bitcast.4, bf16[3584,512]{1,0:T(8,128)(2,1)} %down_h.1, f32[32,2048]{1,0:T(8,128)} %get-tuple-element.11.master, ...), custom_call_target="tpu_custom_call" | custom-call | tf_op jit(solution)/shard_map/pallas_call | solution.py:350

commit v4 on v3

--- a/solution.py
+++ b/solution.py
@@ -184,7 +184,7 @@
             ))
 
     def gather(zz, xx, cc, k, s, r, peer):
-        block = rep.at[at(zz, xx, cc), :, pl.ds(k * W, W)]
+        block = rep.at[k, zz, xx, cc]
         return send(block, block, s, r, peer)
 
     agz, agx, agc = [], [], []
@@ -200,13 +200,17 @@
             master[:, cols], first[:, cols], second[:, cols], total
         )
         new_master[:, cols] = fresh
-        rep[me, :, cols] = fresh.astype(jnp.bfloat16)
+        rep[k, z, x, c] = fresh.astype(jnp.bfloat16)
         agz.append([
             gather(z, x, c, k, agz_s.at[k, d - 1], agz_r.at[k, d - 1], {"dp": at(z_to[d], x, c)})
             for d in range(1, Z)
         ])
         agx.append([gather(z, x, c, k, agx_s.at[k, 0], agx_r.at[k, 0], x_peer)])
-        agc.append([gather(z, x, c, k, agc_s.at[k, 0], agc_r.at[k, 0], core_peer)])
+        agc.append([])
+
+    def whole_core(k, xx, i):
+        block = rep.at[k, :, xx, c]
+        agc[k].append(send(block, block, agc_s.at[k, i], agc_r.at[k, i], core_peer))
 
     def forward(k):
         for d in range(1, Z):
@@ -214,16 +218,12 @@
             agx[k].append(
                 gather(z_from[d], x, c, k, agx_s.at[k, d], agx_r.at[k, d], x_peer)
             )
-            agc[k].append(
-                gather(z_from[d], x, c, k, agc_s.at[k, d], agc_r.at[k, d], core_peer)
-            )
+        whole_core(k, x, 0)
 
     def forward_core(k):
         for d in range(Z):
             agx[k][d].wait_recv()
-            agc[k].append(gather(
-                z_from[d], 1 - x, c, k, agc_s.at[k, Z + d], agc_r.at[k, Z + d], core_peer
-            ))
+        whole_core(k, 1 - x, 1)
 
     for copy in loads[3:]:
         copy.wait()
@@ -273,7 +273,14 @@
         (rep, rep_v, rep_h), (master, master_v, master_h),
         (first, first_v, first_h), (second, second_v, second_h),
     )
-    arrivals = [pltpu.make_async_copy(a, v, in_s.at[i]) for i, (a, v, _) in enumerate(trips)]
+    arrivals = [
+        pltpu.make_async_copy(a, v, in_s.at[i]) for i, (a, v, _) in enumerate(trips[1:])
+    ]
+    K, _, W = rep.shape
+    arrivals += [
+        pltpu.make_async_copy(rep.at[k], rep_v.at[:, pl.ds(k * W, W)], in_s.at[3 + k])
+        for k in range(K)
+    ]
     for copy in arrivals:
         copy.start()
     copies = []
@@ -286,8 +293,9 @@
         ))
         copies[-1].start()
         if n == 0:
+            for copy in arrivals:
+                copy.wait()
             for i, (_, v, b) in enumerate(trips):
-                arrivals[i].wait()
                 copies.append(pltpu.make_async_copy(v, b, out_s.at[i]))
                 copies[-1].start()
     for copy in copies:
@@ -310,7 +318,7 @@
         out_shape=(
             jax.ShapeDtypeStruct((T, half, width), bf16),
             state, state, state,
-            jax.ShapeDtypeStruct((dp, rows, columns), bf16),
+            jax.ShapeDtypeStruct((K, Z, 2, 2, rows, W), bf16),
         ),
         in_specs=[pl.BlockSpec(memory_space=pltpu.HBM)] * 7,
         out_specs=(vmem,) * 5,
@@ -338,7 +346,7 @@
             DMA((T - 1,)), DMA((T - 1,)), DMA((T - 1,)), DMA((T - 1,)),
             DMA((K, Z - 1)), DMA((K, Z - 1)),
             DMA((K, Z)), DMA((K, Z)),
-            DMA((K, 2 * Z)), DMA((K, 2 * Z)),
+            DMA((K, 2)), DMA((K, 2)),
         ],
         compiler_params=pltpu.CompilerParams(
             collective_id=0, has_side_effects=True, vmem_limit_bytes=58 * 1024 * 1024
@@ -365,12 +373,12 @@
             pltpu.VMEM((rows, columns), f32),
             pltpu.VMEM((rows, columns), f32),
             pltpu.VMEM((rows, columns), f32),
-            DMA((4,)),
+            DMA((3 + K,)),
         ],
         compiler_params=pltpu.CompilerParams(vmem_limit_bytes=60 * 1024 * 1024),
     )(
         grad_pre.reshape(tokens, width), down_weight, new_master, new_first, new_second,
-        replica.reshape(dp * rows, columns),
+        replica.reshape(K, dp * rows, W),
     )
 
 

time: 53 us -> 52.6 us (level)
  no operation moved by 1% of the time
where the time goes in v4:
time: 52.6 us; the launch traced here: 52.4 us
  Pallas kernels  51.8 us (98%)
  between operations  0.64 us (1%)
    pallas_call x1, Pallas kernels, local(): pl.pallas_call(functools.partial(kernel, Z, T, K), out_shape=(jax.ShapeDt...  44.8 us
    pallas_call x1, Pallas kernels, local(): pl.pallas_call(finish, out_shape=(jax.ShapeDtypeStruct((tokens, model), b...  7.03 us

profile of v4, /device:TPU:1, one launch (start us, length us, event | category | flops | bytes accessed | tf_op | source)
XLA Modules:
  0.0 52.4 jit_solution(1687813623215251867)
XLA Ops:
  0.6 44.8 %shard_map.119 = (bf16[2,256,512]{2,1,0:T(8,128)(2,1)}, f32[32,2048]{1,0:T(8,128)}, f32[32,2048]{1,0:T(8,128)}, f32[32,2048]{1,0:T(8,128)}, bf16[4,4,2,2,32,512]{5,4,3,2,1,0:T(8,128)(2,1)}) custom-call(bf16[512,512]{1,0:T(8,128)(2,1)} %latent_h.1, f32[1,512]{1,0:T(1,128)} %bitcast.5, bf16[512,2048]{1,0:T(8,128)(2,1)} %kvw_h.1, bf16[512,2048]{1,0:T(8,128)(2,1)} %gkv_h.1, ...), custom_call_target="tpu_custom_call" | custom-call | tf_op jit(solution)/shard_map/pallas_call | solution.py:316
  45.4 7.0 %shard_map.120 = (bf16[512,3584]{1,0:T(8,128)(2,1)}, f32[32,2048]{1,0:T(8,128)}, f32[32,2048]{1,0:T(8,128)}, f32[32,2048]{1,0:T(8,128)}, bf16[512,2048]{1,0:T(8,128)(2,1)}) custom-call(bf16[512,512]{1,0:T(8,128)(2,1)} %bitcast.4, bf16[3584,512]{1,0:T(8,128)(2,1)} %down_h.1, f32[32,2048]{1,0:T(8,128)} %get-tuple-element.11.master, ...), custom_call_target="tpu_custom_call" | custom-call | tf_op jit(solution)/shard_map/pallas_call | solution.py:358
